TPU v7x, 512 devices: a whole 4x4x16 slice. The times are simulated.
512 devices in a mesh: dp: 32 (over z, core), fsdp: 16 (over x, y).
Axes of the slice: x: 4, y: 4, z: 16, core: 2. Of those that a mesh axis runs over, the one named last changes fastest.
Arguments:
- token_ids: int32 [65536], P(('dp', 'fsdp')), may hold values from 0 to 50431, as said below
- activations: bfloat16 [65536, 3072], P(('dp', 'fsdp'))
- grad_out: bfloat16 [65536, 3072], P(('dp', 'fsdp')), may hold values from -0.13183594 to 0.13183594
- error_buffer: bfloat16 [32, 3072, 3072], P('dp', 'fsdp'), may hold values from -6 to 6
- init_q: float32 [3072, 8], replicated, may hold values from -6 to 6
Outputs:
- p_factor: float32 [3072, 8], P('fsdp')
- q_factor: float32 [3072, 8], replicated
- error_next: bfloat16 [32, 3072, 3072], P('dp', 'fsdp')
Inputs may be any that keep to these rules, and one draw needn't show every extreme that they name: `token_ids`: id 1 is padding; on the rows of each device it forms a tail (possibly empty), and each device's first row holds id 0.
All inputs are finite; a program needn't handle non-finite values.
Results may differ from a plain program's by a relative error of at most 0.0006.
Values may be sent and summed in bfloat16 or wider, within the bound.
No kernel may reach another device: no remote copies, remote signals or barrier semaphores. Data moves between devices by JAX's collectives and lax.ppermute only.
A program may use at most 64 MiB of HBM per device.

v0:
```python
import jax
import jax.numpy as jnp
from jax import lax
from jax.sharding import PartitionSpec as P


def orthonormal_columns(p_rows):
    highest = lax.Precision.HIGHEST
    finished = []
    for index_col in range(p_rows.shape[1]):
        column = p_rows[:, index_col]
        if finished:
            stacked = jnp.stack(finished, axis=1)
            inner_vals = lax.psum(jnp.dot(column, stacked, precision=highest), "fsdp")
            column = column - jnp.dot(stacked, inner_vals, precision=highest)
        norm_square = lax.psum(jnp.sum(column * column), "fsdp")
        finished.append(column / jnp.sqrt(norm_square))
    return jnp.stack(finished, axis=1)


def on_device(token_ids, activations, grad_out, error_buffer, init_q):
    highest = lax.Precision.HIGHEST
    replicas = lax.axis_size("dp")
    valid_rows = (token_ids != 1).astype(grad_out.dtype)
    masked_grad = grad_out * valid_rows[:, None]
    x_cols = lax.all_to_all(activations, "fsdp", split_axis=1, concat_axis=0, tiled=True)
    error_rows = error_buffer[0]
    grad_rows = lax.dot_general(
        x_cols,
        lax.all_gather(masked_grad, "fsdp", axis=0, tiled=True),
        (((0,), (0,)), ((), ())),
        preferred_element_type=jnp.float32,
    )
    merged = grad_rows + error_rows.astype(jnp.float32)
    p_local = jnp.dot(merged, init_q, precision=highest)
    p_mean = lax.psum(p_local, "dp") / replicas
    ortho_basis = orthonormal_columns(p_mean)
    q_local = jnp.einsum(
        "rd,rk->dk", merged, ortho_basis, precision=highest, preferred_element_type=jnp.float32
    )
    q_factor = lax.psum(q_local, ("dp", "fsdp")) / replicas
    error_next = (merged - jnp.dot(ortho_basis, q_factor.T, precision=highest)).astype(jnp.bfloat16)
    return (ortho_basis, q_factor, error_next[None])


def solution(mesh):
    return jax.shard_map(
        on_device,
        mesh=mesh,
        in_specs=(
            P(("dp", "fsdp")),
            P(("dp", "fsdp"), None),
            P(("dp", "fsdp"), None),
            P("dp", "fsdp", None),
            P(),
        ),
        out_specs=(P("fsdp", None), P(), P("dp", "fsdp", None)),
        check_vma=False,
    )
```

profile of v0, /device:TPU:1, one launch (start us, length us, event | category | flops | bytes accessed | tf_op | source)
XLA Modules:
  0.0 1197.7 jit_solution(5980001329945168853)
XLA Ops:
  7.2 0.7 compare_convert_fusion
  8.0 2.1 broadcast_multiply_fusion
  10.2 0.4 copy.8
  10.6 19.1 %all_to_all.19 = bf16[128,16,192]{0,2,1:T(8,128)(2,1)S(1)} all-to-all(bf16[128,16,192]{0,2,1:T(8,128)(2,1)S(1)} %bitcast.83), channel_id=1, replica_groups=mesh['dp'=32,'fsdp'=16] {'fsdp'}, dimensions={1} | all-to-all | bytes 1572864 | tf_op jit(solution)/shard_map/all_to_all | solution.py:26
  29.7 92.6 %all-gather.2.cloned.1.call-done = bf16[2048,3072]{1,0:T(8,128)(2,1)} async-done(((bf16[128,3072]{1,0:T(8,128)(2,1)}), bf16[2048,3072]{1,0:T(8,128)(2,1)}) %all-gather.2.cloned.1.call-update) | async-done | bytes 12582928 | tf_op jit(solution)/shard_map/all_gather | solution.py:30
  122.3 7.6 fusion
  130.0 1.9 fusion.29
  131.9 48.0 %psum.119 = f32[192,8]{0,1:T(8,128)S(1)} all-reduce(f32[192,8]{0,1:T(8,128)S(1)} %fusion.29), channel_id=1, replica_groups=mesh['dp'=32,'fsdp'=16] {'dp'}, use_global_device_ids=true, to_apply=%region_0.0 | all-reduce | flops 1536 | bytes 12288 | tf_op jit(solution)/shard_map/psum | solution.py:36
  179.9 0.6 multiply_reduce_fusion.8
  180.5 31.8 %psum.120 = f32[]{:T(128)} all-reduce(f32[]{:T(128)} %multiply_reduce_fusion.8), channel_id=1, replica_groups=mesh['dp'=32,'fsdp'=16] {'fsdp'}, use_global_device_ids=true, to_apply=%region_2.0 | all-reduce | flops 1 | bytes 8 | tf_op jit(solution)/shard_map/psum | solution.py:16
  213.0 0.6 multiply_reduce_fusion
  213.6 29.1 %psum.121 = f32[]{:T(128)} all-reduce(f32[]{:T(128)} %multiply_reduce_fusion), channel_id=1, replica_groups=mesh['dp'=32,'fsdp'=16] {'fsdp'}, use_global_device_ids=true, to_apply=%region_3.0 | all-reduce | flops 1 | bytes 8 | tf_op jit(solution)/shard_map/psum | solution.py:14
  242.8 1.2 multiply_reduce_fusion.7
  244.0 30.6 %psum.122 = f32[]{:T(128)} all-reduce(f32[]{:T(128)} %multiply_reduce_fusion.7), channel_id=1, replica_groups=mesh['dp'=32,'fsdp'=16] {'fsdp'}, use_global_device_ids=true, to_apply=%region_5.0 | all-reduce | flops 1 | bytes 8 | tf_op jit(solution)/shard_map/psum | solution.py:16
  275.3 0.7 broadcast_divide_fusion.6
  275.9 0.1 convolution_bitcast_fusion.6
  276.1 29.1 %psum.123 = f32[2]{0:T(128)S(1)} all-reduce(f32[2]{0:T(128)S(1)} %convolution_bitcast_fusion.6), channel_id=1, replica_groups=mesh['dp'=32,'fsdp'=16] {'fsdp'}, use_global_device_ids=true, to_apply=%region_6.0 | all-reduce | flops 2 | bytes 16 | tf_op jit(solution)/shard_map/psum | solution.py:14
  305.1 0.1 fusion.7
  305.3 0.6 multiply_reduce_fusion.6
  305.9 30.0 %psum.124 = f32[]{:T(128)} all-reduce(f32[]{:T(128)} %get-tuple-element.13), channel_id=1, replica_groups=mesh['dp'=32,'fsdp'=16] {'fsdp'}, use_global_device_ids=true, to_apply=%region_8.0 | all-reduce | flops 1 | bytes 8 | tf_op jit(solution)/shard_map/psum | solution.py:16
  336.6 0.1 convolution_bitcast_fusion.5
  336.7 29.1 %psum.125 = f32[3]{0:T(128)S(1)} all-reduce(f32[3]{0:T(128)S(1)} %convolution_bitcast_fusion.5), channel_id=1, replica_groups=mesh['dp'=32,'fsdp'=16] {'fsdp'}, use_global_device_ids=true, to_apply=%region_9.0 | all-reduce | flops 3 | bytes 24 | tf_op jit(solution)/shard_map/psum | solution.py:14
  365.8 0.1 fusion.5
  365.9 0.6 multiply_reduce_fusion.5
  366.5 30.0 %psum.126 = f32[]{:T(128)} all-reduce(f32[]{:T(128)} %get-tuple-element.11), channel_id=1, replica_groups=mesh['dp'=32,'fsdp'=16] {'fsdp'}, use_global_device_ids=true, to_apply=%region_11.0 | all-reduce | flops 1 | bytes 8 | tf_op jit(solution)/shard_map/psum | solution.py:16
  397.2 0.1 convolution_bitcast_fusion.4
  397.3 29.5 %psum.127 = f32[4]{0:T(128)S(1)} all-reduce(f32[4]{0:T(128)S(1)} %convolution_bitcast_fusion.4), channel_id=1, replica_groups=mesh['dp'=32,'fsdp'=16] {'fsdp'}, use_global_device_ids=true, to_apply=%region_12.0 | all-reduce | flops 4 | bytes 32 | tf_op jit(solution)/shard_map/psum | solution.py:14
  426.8 0.1 fusion.6
  427.0 0.6 multiply_reduce_fusion.4
  427.6 29.6 %psum.128 = f32[]{:T(128)} all-reduce(f32[]{:T(128)} %get-tuple-element.9), channel_id=1, replica_groups=mesh['dp'=32,'fsdp'=16] {'fsdp'}, use_global_device_ids=true, to_apply=%region_14.0 | all-reduce | flops 1 | bytes 8 | tf_op jit(solution)/shard_map/psum | solution.py:16
  457.9 0.1 convolution_bitcast_fusion.3
  458.0 29.8 %psum.129 = f32[5]{0:T(128)S(1)} all-reduce(f32[5]{0:T(128)S(1)} %convolution_bitcast_fusion.3), channel_id=1, replica_groups=mesh['dp'=32,'fsdp'=16] {'fsdp'}, use_global_device_ids=true, to_apply=%region_15.0 | all-reduce | flops 5 | bytes 40 | tf_op jit(solution)/shard_map/psum | solution.py:14
  487.8 0.1 fusion.12
  487.9 0.6 multiply_reduce_fusion.3
  488.5 29.3 %psum.130 = f32[]{:T(128)} all-reduce(f32[]{:T(128)} %get-tuple-element.7), channel_id=1, replica_groups=mesh['dp'=32,'fsdp'=16] {'fsdp'}, use_global_device_ids=true, to_apply=%region_17.0 | all-reduce | flops 1 | bytes 8 | tf_op jit(solution)/shard_map/psum | solution.py:16
  518.5 0.1 convolution_bitcast_fusion.2
  518.7 30.6 %psum.131 = f32[6]{0:T(128)S(1)} all-reduce(f32[6]{0:T(128)S(1)} %convolution_bitcast_fusion.2), channel_id=1, replica_groups=mesh['dp'=32,'fsdp'=16] {'fsdp'}, use_global_device_ids=true, to_apply=%region_18.0 | all-reduce | flops 6 | bytes 48 | tf_op jit(solution)/shard_map/psum | solution.py:14
  549.3 0.1 fusion.10
  549.4 0.6 multiply_reduce_fusion.2
  550.0 29.3 %psum.132 = f32[]{:T(128)} all-reduce(f32[]{:T(128)} %get-tuple-element.5), channel_id=1, replica_groups=mesh['dp'=32,'fsdp'=16] {'fsdp'}, use_global_device_ids=true, to_apply=%region_20.0 | all-reduce | flops 1 | bytes 8 | tf_op jit(solution)/shard_map/psum | solution.py:16
  580.1 0.1 convolution_bitcast_fusion.1
  580.2 30.5 %psum.133 = f32[7]{0:T(128)S(1)} all-reduce(f32[7]{0:T(128)S(1)} %convolution_bitcast_fusion.1), channel_id=1, replica_groups=mesh['dp'=32,'fsdp'=16] {'fsdp'}, use_global_device_ids=true, to_apply=%region_21.0 | all-reduce | flops 7 | bytes 56 | tf_op jit(solution)/shard_map/psum | solution.py:14
  610.9 0.6 multiply_reduce_fusion.1
  611.5 29.1 %psum.134 = f32[]{:T(128)} all-reduce(f32[]{:T(128)} %get-tuple-element.3), channel_id=1, replica_groups=mesh['dp'=32,'fsdp'=16] {'fsdp'}, use_global_device_ids=true, to_apply=%region_23.0 | all-reduce | flops 1 | bytes 8 | tf_op jit(solution)/shard_map/psum | solution.py:16
  641.3 2.0 fusion.30
  643.3 543.5 %all-reduce.2.cloned.1.call-done = f32[3072,8]{0,1:T(8,128)} async-done(((f32[3072,8]{0,1:T(8,128)}), f32[3072,8]{0,1:T(8,128)}) %all-reduce.2.cloned.1.call-update) | async-done | bytes 98320 | tf_op jit(solution)/shard_map/psum | solution.py:41
  1186.9 0.9 broadcast_multiply_fusion.1
  1187.8 3.1 fusion.2
  (25 shorter events, 0.4 us)
Async XLA Ops:
  7.2 122.8 %copy-start = (f32[3072,8]{0,1:T(8,128)S(1)}, f32[3072,8]{0,1:T(8,128)}, u32[]{:S(2)}) copy-start(f32[3072,8]{0,1:T(8,128)} %param.9) | copy-start | bytes 294916
  7.2 3.0 copy-start.1
  7.2 115.1 %all-gather.2.cloned.1.call-start = ((), (), s32[]{:S(2)}) async-start(), calls=%async_computation.1 | async-start | bytes 13369344 | tf_op jit(solution)/shard_map/all_gather | solution.py:30
  10.1 1176.7 %all-reduce.2.cloned.1.call-start = ((), (), s32[]{:S(2)}) async-start(), calls=%async_computation.2 | async-start | bytes 196608 | tf_op jit(solution)/shard_map/psum | solution.py:41
  641.3 549.5 %copy-start.3 = (f32[192,8]{0,1:T(8,128)}, f32[192,8]{0,1:T(8,128)S(1)}, u32[]{:S(2)}) copy-start(f32[192,8]{0,1:T(8,128)S(1)} %stack.41) | copy-start | bytes 18436
  1187.8 3.1 copy-start.2
Sparse Core Ops, SparseCore 0:
  11.7 110.6 all-gather.1
  643.4 543.3 all-reduce.1
where the time goes:
time: 1200 us
  waiting for transfers between devices  636 us (53%)
  blocking collectives  514 us (43%)
  between operations  19.7 us (2%)
  matrix products  16.2 us (1%)
    psum x1, waiting for transfers between devices, on_device(): q_factor = lax.psum(q_local, ('dp', 'fsdp')) / replicas  544 us
    psum x8, blocking collectives, orthonormal_columns(): norm_square = lax.psum(jnp.sum(column * column), 'fsdp')  240 us
    psum x7, blocking collectives, orthonormal_columns(): inner_vals = lax.psum(jnp.dot(column, stacked, precision=highest), 'fsdp')  208 us
    all_gather x1, waiting for transfers between devices, on_device(): lax.all_gather(masked_grad, 'fsdp', axis=0, tiled=True)  92.6 us
    psum x1, blocking collectives, on_device(): p_mean = lax.psum(p_local, 'dp') / replicas  48 us
  transfers between devices with their start and end apart: 2, of which 2 were waited for; matrix products, arithmetic and copies ran while one was open for 0% of the time, Pallas kernels for 0%

commit v1 on v0

v1 whole, which is shorter than its diff:
```python
import math

import jax
import jax.numpy as jnp
from jax import lax
from jax.experimental import pallas as pl
from jax.experimental.pallas import tpu as pltpu
from jax.sharding import Mesh, PartitionSpec as P

RANK = 8
F32, BF16 = jnp.float32, jnp.bfloat16
ROWS_OF_SPLIT = 4 * RANK
NT = (((1,), (1,)), ((), ()))
TN = (((0,), (0,)), ((), ()))
XP_SCALE = 2.0**-8


def terms(value):
    high = value.astype(BF16).astype(F32)
    rest = value - high
    middle = rest.astype(BF16).astype(F32)
    return high, middle, rest - middle


def split(value):
    return jnp.concatenate([*terms(value), jnp.zeros_like(value)], axis=0).astype(BF16)


def join(value):
    return value[:RANK] + value[RANK : 2 * RANK] + value[2 * RANK : 3 * RANK]


def dot(a, b, dims=(((1,), (0,)), ((), ()))):
    return lax.dot_general(a, b, dims, preferred_element_type=F32)


def lanes(ref, rows=slice(None)):
    return jnp.concatenate([ref[i, rows, :] for i in range(ref.shape[0])], axis=1)


def call(kernel, out_shape, *args, flops=0):
    nbytes = sum(math.prod(a.shape) * a.dtype.itemsize for a in args)
    return pl.pallas_call(
        kernel,
        out_shape=out_shape,
        in_specs=[pl.BlockSpec(memory_space=pltpu.VMEM)] * len(args),
        out_specs=jax.tree.map(lambda _: pl.BlockSpec(memory_space=pltpu.VMEM), out_shape),
        compiler_params=pltpu.CompilerParams(vmem_limit_bytes=40 * 2**20),
        cost_estimate=pl.CostEstimate(flops=flops, bytes_accessed=nbytes, transcendentals=0),
    )(*args)


def pack_kernel(ids_ref, x_ref, g_ref, initq_ref, pay_ref):
    parts, rows, _ = pay_ref.shape
    width = rows - ROWS_OF_SPLIT
    valid = (ids_ref[...] != 1).astype(F32)
    gq = join(dot(split(initq_ref[...]), g_ref[...], NT))
    gq = split(gq * valid)
    for i in range(parts):
        block = x_ref[:, i * width : (i + 1) * width].astype(F32).T * valid
        pay_ref[i, :width, :] = block.astype(BF16)
        pay_ref[i, width:, :] = gq


def left_kernel(recv_ref, e_ref, initq_ref, p_ref):
    width = recv_ref.shape[1] - ROWS_OF_SPLIT
    x_cols = lanes(recv_ref, slice(0, width))
    gq = lanes(recv_ref, slice(width, None))
    p_ref[...] = join(dot(gq, x_cols, NT)) + join(dot(split(initq_ref[...]), e_ref[...], NT))


def inverse_factor(gram):
    eye = (lax.broadcasted_iota(jnp.int32, gram.shape, 0) == lax.broadcasted_iota(jnp.int32, gram.shape, 1)).astype(F32)
    row = lax.broadcasted_iota(jnp.int32, (RANK, 1), 0)
    left, right = gram, eye
    scale = jnp.zeros((RANK, 1), F32)
    for k in range(RANK):
        pivot = left[k : k + 1, k : k + 1]
        factor = jnp.where(row > k, left[:, k : k + 1] / pivot, 0.0)
        scale = jnp.where(row == k, lax.rsqrt(pivot), scale)
        next_left = left - factor * left[k : k + 1, :]
        right = right - factor * right[k : k + 1, :]
        left = next_left
    return right * scale


def right_kernel(pfull_ref, pown_ref, pay_ref, g_ref, e_ref, pout_ref, q_ref):
    parts, _, width = pfull_ref.shape
    high = dict(precision=lax.Precision.HIGHEST, preferred_element_type=F32)
    p_full = lanes(pfull_ref)
    gram = lax.dot_general(p_full, p_full, NT, **high)
    inverse = inverse_factor(gram)
    factor = jnp.dot(inverse, p_full, **high)
    own = jnp.dot(inverse, pown_ref[...], **high)
    pout_ref[...] = own
    small = split(factor * XP_SCALE)
    x_rows = jnp.concatenate([pay_ref[i, :width, :] for i in range(parts)], axis=0)
    xp = split(join(dot(small, x_rows)))
    q = join(dot(xp, g_ref[...])) * (1.0 / XP_SCALE) + join(dot(split(own), e_ref[...]))
    for i in range(parts):
        q_ref[i] = q[:, i * width : (i + 1) * width]


def final_kernel(recv_ref, g_ref, e_ref, p_ref, q_ref, out_ref):
    width = recv_ref.shape[1] - ROWS_OF_SPLIT
    p_high, p_middle, p_low = terms(p_ref[...])
    q_high, q_middle, q_low = terms(q_ref[...])
    p_terms = jnp.concatenate([p_high, p_high, p_middle, p_high, p_low, p_middle], axis=0).astype(BF16)
    q_terms = jnp.concatenate([q_high, q_middle, q_high, q_low, q_high, q_middle], axis=0).astype(BF16)
    merged = dot(lanes(recv_ref, slice(0, width)), g_ref[...]) + e_ref[...].astype(F32)
    out_ref[...] = (merged - dot(p_terms, q_terms, TN)).astype(BF16)


def final(recv, g_all, error_rows, p_own, q_full):
    parts, rows, tokens = recv.shape
    width, columns = error_rows.shape
    tile = math.gcd(columns, 384)
    return pl.pallas_call(
        final_kernel,
        out_shape=jax.ShapeDtypeStruct((width, columns), BF16),
        grid=(columns // tile,),
        in_specs=[
            pl.BlockSpec((parts, rows, tokens), lambda j: (0, 0, 0)),
            pl.BlockSpec((parts * tokens, tile), lambda j: (0, j)),
            pl.BlockSpec((width, tile), lambda j: (0, j)),
            pl.BlockSpec((RANK, width), lambda j: (0, 0)),
            pl.BlockSpec((RANK, tile), lambda j: (0, j)),
        ],
        out_specs=pl.BlockSpec((width, tile), lambda j: (0, j)),
        compiler_params=pltpu.CompilerParams(vmem_limit_bytes=40 * 2**20),
        cost_estimate=pl.CostEstimate(
            flops=2 * width * columns * parts * tokens,
            bytes_accessed=2 * columns * (parts * tokens + 2 * width),
            transcendentals=0,
        ),
    )(recv, g_all, error_rows, p_own, q_full)


def exchange(value, axes):
    return lax.all_to_all(value, axes, split_axis=0, concat_axis=0, tiled=True)


def gather(value, axes, parts):
    return exchange(jnp.broadcast_to(value[None], (parts, *value.shape)), axes)


def on_device(token_ids, activations, grad_out, error_buffer, init_q):
    plane = ("x", "y")
    parts = lax.axis_size(plane)
    depth = lax.axis_size("z")
    replicas = depth * lax.axis_size("core")
    tokens, features = activations.shape
    width = features // parts
    columns = grad_out.shape[1]
    error_rows = error_buffer[0]
    initq_t = init_q.T

    def over_replicas(value):
        return jnp.sum(gather(lax.psum(value, "core"), "z", depth), axis=0) / replicas

    g_all = lax.all_gather(grad_out, plane, axis=0, tiled=True)
    payload = call(
        pack_kernel,
        jax.ShapeDtypeStruct((parts, width + ROWS_OF_SPLIT, tokens), BF16),
        token_ids[None], activations, grad_out, initq_t,
    )
    recv = exchange(payload, plane)
    p_local = call(left_kernel, jax.ShapeDtypeStruct((RANK, width), F32), recv, error_rows, initq_t)
    p_mean = over_replicas(p_local)
    p_full = gather(p_mean, plane, parts)
    p_own, q_terms = call(
        right_kernel,
        (
            jax.ShapeDtypeStruct((RANK, width), F32),
            jax.ShapeDtypeStruct((parts, RANK, columns // parts), F32),
        ),
        p_full, p_mean, payload, grad_out, error_rows,
    )
    q_own = over_replicas(jnp.sum(exchange(q_terms, plane), axis=0))
    q_full = gather(q_own, plane, parts).swapaxes(0, 1).reshape(RANK, columns)
    error_next = final(recv, g_all, error_rows, p_own, q_full)
    return p_own.T, q_full.T, error_next[None]


def solution(mesh):
    replicas, parts = mesh.shape["dp"], mesh.shape["fsdp"]
    side = math.isqrt(parts)
    fine = Mesh(mesh.devices.reshape(replicas // 2, 2, side, parts // side), ("z", "core", "x", "y"))
    everywhere = ("z", "core", "x", "y")
    return jax.shard_map(
        on_device,
        mesh=fine,
        in_specs=(
            P(everywhere),
            P(everywhere, None),
            P(everywhere, None),
            P(("z", "core"), ("x", "y"), None),
            P(),
        ),
        out_specs=(P(("x", "y"), None), P(), P(("z", "core"), ("x", "y"), None)),
        check_vma=False,
    )
```

time: 1200 us -> 145 us (0.12)
  waiting for transfers between devices: 636 us -> 0.7 us
  blocking collectives: 514 us -> 110 us
  matrix products: 16.2 us -> 0 us
  Pallas kernels: 0 us -> 13.4 us
    psum x1 -> x0, waiting for transfers between devices: 544 us -> none  [on_device(): q_factor = lax.psum(q_local, ('dp', 'fsdp')) / replicas]
    psum x16 -> x2, blocking collectives: 495 us -> 14.1 us  [over_replicas(): lax.psum(value, 'core')]
    all_gather x1, waiting for transfers between devices: 92.6 us -> 0.02 us  [on_device(): g_all = lax.all_gather(grad_out, plane, axis=0, tiled=True)]
    all_to_all x1 -> x6, blocking collectives: 19.1 us -> 96.2 us  [exchange(): return lax.all_to_all(value, axes, split_axis=0, concat_axis=0, tiled=True)]
    dot_general x16 -> x0, matrix products: 16.2 us -> none  [the longest x1 7.62 us: on_device(): lax.dot_general(x_cols, lax.all_gather(masked_grad, 'fsdp', axis=0, tiled...]
    pallas_call x0 -> x4, Pallas kernels: none -> 13.4 us  [the longest x1 9.95 us: final(): pl.pallas_call(final_kernel, out_shape=jax.ShapeDtypeStruct((width, colum...]
  transfers between devices with their start and end apart: 2 -> 1, of which waited for: 2 -> 0; matrix products, arithmetic and copies ran while one was open for 0% -> 0% of each run, Pallas kernels for 0% -> 2%
where the time goes in v1:
time: 145 us; the launch traced here: 143 us
  blocking collectives  110 us (76%)
  between operations  14.1 us (10%)
  Pallas kernels  13.4 us (9%)
  local copies, waits for them, and re-layouts  4.46 us (3%)
    all_to_all x6, blocking collectives, exchange(): return lax.all_to_all(value, axes, split_axis=0, concat_axis=0, tiled=True)  96.2 us
    psum x2, blocking collectives, over_replicas(): lax.psum(value, 'core')  14.1 us
    pallas_call x1, Pallas kernels, final(): pl.pallas_call(final_kernel, out_shape=jax.ShapeDtypeStruct((width, colum...  9.95 us
    unnamed x18, local copies, waits for them, and re-layouts  4.26 us
    pallas_call x3, Pallas kernels, call(): pl.pallas_call(kernel, out_shape=out_shape, in_specs=[pl.BlockSpec(memory...  3.5 us
  transfers between devices with their start and end apart: 1, of which 0 were waited for; matrix products, arithmetic and copies ran while one was open for 0% of the time, Pallas kernels for 2%

profile of v1, /device:TPU:1, one launch (start us, length us, event | category | flops | bytes accessed | tf_op | source)
XLA Modules:
  0.0 143.2 jit_solution(11252444131663713130)
XLA Ops:
  7.2 0.0 copy-start.1
  7.2 0.0 all-gather.2.cloned.1.call-start
  7.2 0.7 all-gather.2.cloned.1.call-update
  7.9 0.4 copy-done.1
  8.3 0.0 copy-start.3
  8.3 1.1 copy-done.3
  9.4 0.0 copy-start.5
  9.4 0.9 copy-done.5
  10.3 0.0 copy-start.8
  10.3 0.7 copy-done.8
  11.0 0.6 shard_map.76.pay_ref
  11.6 0.0 copy-start
  11.6 0.0 copy-start.6
  11.6 20.3 %all_to_all.30.recv_ref = bf16[16,224,128]{2,1,0:T(8,128)(2,1)S(1)} all-to-all(bf16[16,224,128]{2,1,0:T(8,128)(2,1)S(1)} %shard_map.76.pay_ref), channel_id=1, replica_groups=mesh['z'=16,'core'=2,'x'=4,'y'=4] {'x','y'}, dimensions={0} | all-to-all | bytes 1835008 | tf_op jit(solution)/shard_map/all_to_all | solution.py:140
  31.9 0.0 copy-done
  31.9 0.0 copy-done.6
  31.9 0.7 shard_map.77
  32.6 5.8 %psum.14 = f32[8,192]{1,0:T(8,128)S(1)} all-reduce(f32[8,192]{1,0:T(8,128)S(1)} %shard_map.77), channel_id=1, replica_groups=mesh['z'=16,'core'=2,'x'=4,'y'=4] {'core'}, use_global_device_ids=true, to_apply=%region_0.0 | all-reduce | flops 1536 | bytes 12288 | tf_op jit(solution)/shard_map/psum | solution.py:159
  38.4 26.9 %all_to_all.31 = f32[16,8,192]{2,1,0:T(8,128)S(1)} all-to-all(f32[16,8,192]{2,1,0:T(8,128)S(1)} %broadcast_in_dim.13), channel_id=1, replica_groups=mesh['z'=16,'core'=2,'x'=4,'y'=4] {'z'}, dimensions={0} | all-to-all | bytes 196608 | tf_op jit(solution)/shard_map/all_to_all | solution.py:140
  65.3 10.9 %all_to_all.32.pfull_ref = f32[16,8,192]{2,1,0:T(8,128)S(1)} all-to-all(f32[16,8,192]{2,1,0:T(8,128)S(1)} %broadcast_in_dim.14), channel_id=1, replica_groups=mesh['z'=16,'core'=2,'x'=4,'y'=4] {'x','y'}, dimensions={0} | all-to-all | bytes 196608 | tf_op jit(solution)/shard_map/all_to_all | solution.py:140
  76.2 0.0 copy-start.2
  76.2 1.2 copy-done.2
  77.4 2.2 %shard_map.78 = (f32[8,192]{1,0:T(8,128)}, f32[16,8,192]{2,1,0:T(8,128)S(1)}) custom-call(f32[16,8,192]{2,1,0:T(8,128)S(1)} %all_to_all.32.pfull_ref, f32[8,192]{1,0:T(8,128)S(1)} %broadcast_multiply_fusion.1.pown_ref, bf16[16,224,128]{2,1,0:T(8,128)(2,1)S(1)} %shard_map.76.pay_ref, bf16[128,3072]{1,0:T(8,128)(2,1)S(1)} %copy-done.2, ...), custom_call_target="tpu_custom_call" | custom-call | bytes 2988032 | tf_op jit(solution)/shard_map/pallas_call | solution.py:43
  79.5 0.0 copy-start.7
  79.5 11.3 %all_to_all.33 = f32[16,8,192]{2,1,0:T(8,128)S(1)} all-to-all(f32[16,8,192]{2,1,0:T(8,128)S(1)} %get-tuple-element.6), channel_id=1, replica_groups=mesh['z'=16,'core'=2,'x'=4,'y'=4] {'x','y'}, dimensions={0} | all-to-all | bytes 196608 | tf_op jit(solution)/shard_map/all_to_all | solution.py:140
  90.9 8.3 %psum.15 = f32[8,192]{1,0:T(8,128)S(1)} all-reduce(f32[8,192]{1,0:T(8,128)S(1)} %reduce_sum.28), channel_id=1, replica_groups=mesh['z'=16,'core'=2,'x'=4,'y'=4] {'core'}, use_global_device_ids=true, to_apply=%region_3.0 | all-reduce | flops 1536 | bytes 12288 | tf_op jit(solution)/shard_map/psum | solution.py:159
  99.2 15.7 %all_to_all.34 = f32[16,8,192]{2,1,0:T(8,128)S(1)} all-to-all(f32[16,8,192]{2,1,0:T(8,128)S(1)} %broadcast_in_dim.15), channel_id=1, replica_groups=mesh['z'=16,'core'=2,'x'=4,'y'=4] {'z'}, dimensions={0} | all-to-all | bytes 196608 | tf_op jit(solution)/shard_map/all_to_all | solution.py:140
  115.0 11.2 %all_to_all.35 = f32[16,8,192]{2,1,0:T(8,128)S(1)} all-to-all(f32[16,8,192]{2,1,0:T(8,128)S(1)} %broadcast_in_dim.16), channel_id=1, replica_groups=mesh['z'=16,'core'=2,'x'=4,'y'=4] {'x','y'}, dimensions={0} | all-to-all | bytes 196608 | tf_op jit(solution)/shard_map/all_to_all | solution.py:140
  126.2 0.1 reshape.17.q_ref
  126.3 0.0 copy-start.4
  126.3 0.0 all-gather.2.cloned.1.call-done.g_ref
  126.4 0.0 copy-done.7
  126.4 9.9 %shard_map.79 = bf16[192,3072]{1,0:T(8,128)(2,1)} custom-call(bf16[16,224,128]{2,1,0:T(8,128)(2,1)S(1)} %all_to_all.30.recv_ref, bf16[2048,3072]{1,0:T(8,128)(2,1)} %all-gather.2.cloned.1.call-done.g_ref, bf16[192,3072]{1,0:T(8,128)(2,1)S(1)} %bitcast.9, f32[8,192]{1,0:T(8,128)S(1)} %copy-done.7, f32[8,3072]{1,0:T(8,128)S(1)} %reshape.17.q_ref), custom_call_target="tpu_custom_call" | custom-call | flops 2415919104 | bytes 14942208 | tf_op jit(solution)/shard_map/pallas_call | solution.py:118
  136.3 0.0 copy-done.4
  (10 shorter events, 0.2 us)
Async XLA Ops:
  7.2 1.1 copy-start.1
  7.2 119.2 %all-gather.2.cloned.1.call-start = ((), (), s32[]{:S(2)}) async-start(), calls=%async_computation.6 | async-start | bytes 13369344 | tf_op jit(solution)/shard_map/all_gather | solution.py:161
  8.3 1.1 copy-start.3
  9.4 0.9 copy-start.5
  10.3 0.7 copy-start.8
  11.6 20.3 %copy-start = (bf16[1,192,3072]{2,1,0:T(8,128)(2,1)S(1)}, bf16[1,192,3072]{2,1,0:T(8,128)(2,1)}, u32[]{:S(2)}) copy-start(bf16[1,192,3072]{2,1,0:T(8,128)(2,1)} %param.8) | copy-start | bytes 3538948
  11.6 20.3 %copy-start.6 = (f32[3072,8]{0,1:T(8,128)S(1)}, f32[3072,8]{0,1:T(8,128)}, u32[]{:S(2)}) copy-start(f32[3072,8]{0,1:T(8,128)} %param.9) | copy-start | bytes 294916
  76.2 1.2 copy-start.2
  79.5 46.8 %copy-start.7 = (f32[8,192]{1,0:T(8,128)S(1)}, f32[8,192]{1,0:T(8,128)}, u32[]{:S(2)}) copy-start(f32[8,192]{1,0:T(8,128)} %get-tuple-element.5.p_ref) | copy-start | bytes 18436
  126.3 10.0 %copy-start.4 = (f32[8,3072]{1,0:T(8,128)}, f32[8,3072]{1,0:T(8,128)S(1)}, u32[]{:S(2)}) copy-start(f32[8,3072]{1,0:T(8,128)S(1)} %reshape.17.q_ref) | copy-start | bytes 294916
Sparse Core Ops, SparseCore 0:
  11.1 113.9 all-gather.1

commit v2 on v1

v2 whole, which is shorter than its diff:
```python
import functools
import math

import jax
import jax.numpy as jnp
from jax import lax
from jax.experimental import pallas as pl
from jax.experimental.pallas import tpu as pltpu
from jax.sharding import Mesh, PartitionSpec as P

RANK = 8
LANES = 128
SPLIT_ROWS = 4 * RANK
F32, BF16 = jnp.float32, jnp.bfloat16
NT = (((1,), (1,)), ((), ()))
TN = (((0,), (0,)), ((), ()))
XP_SCALE = 2.0**-8
VMEM = pl.BlockSpec(memory_space=pltpu.VMEM)
ANY = pl.BlockSpec(memory_space=pl.ANY)


def terms(value):
    high = value.astype(BF16).astype(F32)
    rest = value - high
    middle = rest.astype(BF16).astype(F32)
    return high, middle, rest - middle


def split(value):
    return jnp.concatenate([*terms(value), jnp.zeros_like(value)], axis=0).astype(BF16)


def join(value):
    return value[:RANK] + value[RANK : 2 * RANK] + value[2 * RANK : 3 * RANK]


def dot(a, b, dims=(((1,), (0,)), ((), ()))):
    return lax.dot_general(a, b, dims, preferred_element_type=F32)


def stack(value):
    return jnp.concatenate([value[:, i : i + LANES] for i in range(0, value.shape[1], LANES)], axis=0)


def unstack(value):
    return jnp.concatenate([value[i : i + RANK] for i in range(0, value.shape[0], RANK)], axis=1)


def lanes(ref, rows=slice(None)):
    return jnp.concatenate([ref[i, rows, :] for i in range(ref.shape[0])], axis=1)


def call(kernel, out_shape, specs, *args, scratch=(), flops=0):
    nbytes = sum(math.prod(a.shape) * a.dtype.itemsize for a in args)
    return pl.pallas_call(
        kernel,
        out_shape=out_shape,
        in_specs=specs,
        out_specs=jax.tree.map(lambda _: VMEM, out_shape),
        scratch_shapes=scratch,
        compiler_params=pltpu.CompilerParams(vmem_limit_bytes=40 * 2**20),
        cost_estimate=pl.CostEstimate(flops=flops, bytes_accessed=nbytes, transcendentals=0),
    )(*args)


def pack_kernel(ids_hbm, x_hbm, g_hbm, initq_hbm, pay_ref, ids_ref, x_ref, g_ref, initq_ref, sems):
    sources = (initq_hbm, g_hbm, ids_hbm, x_hbm)
    targets = (initq_ref, g_ref, ids_ref, x_ref)
    copies = [pltpu.make_async_copy(*pair, sems.at[i]) for i, pair in enumerate(zip(sources, targets))]
    for copy in copies:
        copy.start()
    for copy in copies[:3]:
        copy.wait()
    parts, rows, _ = pay_ref.shape
    width = rows - SPLIT_ROWS
    valid = (ids_ref[...] != 1).astype(F32)
    gq = split(join(dot(split(initq_ref[...]), g_ref[...], NT)) * valid)
    copies[3].wait()
    for i in range(parts):
        block = x_ref[:, i * width : (i + 1) * width].astype(F32).T * valid
        pay_ref[i, :width, :] = block.astype(BF16)
        pay_ref[i, width:, :] = gq


def left_kernel(recv_ref, e_ref, initq_ref, p_ref):
    width = recv_ref.shape[1] - SPLIT_ROWS
    x_cols = lanes(recv_ref, slice(0, width))
    gq = lanes(recv_ref, slice(width, None))
    p_ref[...] = join(dot(gq, x_cols, NT)) + join(dot(split(initq_ref[...]), e_ref[...], NT))


def inverse_factor(gram):
    eye = (lax.broadcasted_iota(jnp.int32, gram.shape, 0) == lax.broadcasted_iota(jnp.int32, gram.shape, 1)).astype(F32)
    row = lax.broadcasted_iota(jnp.int32, (RANK, 1), 0)
    left, right = gram, eye
    scale = jnp.zeros((RANK, 1), F32)
    for k in range(RANK):
        pivot = left[k : k + 1, k : k + 1]
        factor = jnp.where(row > k, left[:, k : k + 1] / pivot, 0.0)
        scale = jnp.where(row == k, lax.rsqrt(pivot), scale)
        next_left = left - factor * left[k : k + 1, :]
        right = right - factor * right[k : k + 1, :]
        left = next_left
    return right * scale


def right_kernel(pfull_ref, pown_ref, ids_ref, x_ref, g_ref, e_ref, own_ref, q_ref):
    high = dict(precision=lax.Precision.HIGHEST, preferred_element_type=F32)
    p_full = lanes(pfull_ref)
    gram = lax.dot_general(p_full, p_full, NT, **high)
    inverse = inverse_factor(gram)
    factor = jnp.dot(inverse, p_full, **high)
    own = jnp.dot(inverse, pown_ref[...], **high)
    own_ref[...] = own
    valid = ids_ref[...] != 1
    xp = join(dot(split(factor * XP_SCALE), x_ref[...], NT))
    xp = split(jnp.where(valid, xp, 0.0))
    q = join(dot(xp, g_ref[...])) * (1.0 / XP_SCALE) + join(dot(split(own), e_ref[...]))
    q_ref[...] = stack(q)


def final_kernel(replicas, recv_ref, g_ref, e_ref, p_ref, q_ref, out_ref, qout_ref):
    width = out_ref.shape[0]
    q = unstack(q_ref[...]) * (1.0 / replicas)
    qout_ref[...] = q
    p_high, p_middle, p_low = terms(p_ref[...])
    q_high, q_middle, q_low = terms(q)
    p_terms = jnp.concatenate([p_high, p_high, p_middle, p_high, p_low, p_middle], axis=0).astype(BF16)
    q_terms = jnp.concatenate([q_high, q_middle, q_high, q_low, q_high, q_middle], axis=0).astype(BF16)
    merged = dot(lanes(recv_ref, slice(0, width)), g_ref[...]) + e_ref[...].astype(F32)
    out_ref[...] = (merged - dot(p_terms, q_terms, TN)).astype(BF16)


def final(replicas, recv, g_all, error_rows, p_own, q_sum):
    parts, _, tokens = recv.shape
    width, columns = error_rows.shape
    tile = math.gcd(columns, 768)
    return pl.pallas_call(
        functools.partial(final_kernel, replicas),
        out_shape=(jax.ShapeDtypeStruct((width, columns), BF16), jax.ShapeDtypeStruct((RANK, columns), F32)),
        grid=(columns // tile,),
        in_specs=[
            pl.BlockSpec(recv.shape, lambda j: (0, 0, 0)),
            pl.BlockSpec((parts * tokens, tile), lambda j: (0, j)),
            pl.BlockSpec((width, tile), lambda j: (0, j)),
            pl.BlockSpec((RANK, width), lambda j: (0, 0)),
            pl.BlockSpec((tile * RANK // LANES, LANES), lambda j: (j, 0)),
        ],
        out_specs=(pl.BlockSpec((width, tile), lambda j: (0, j)), pl.BlockSpec((RANK, tile), lambda j: (0, j))),
        compiler_params=pltpu.CompilerParams(vmem_limit_bytes=40 * 2**20),
        cost_estimate=pl.CostEstimate(
            flops=2 * width * columns * parts * tokens,
            bytes_accessed=2 * columns * (parts * tokens + 2 * width),
            transcendentals=0,
        ),
    )(recv, g_all, error_rows, p_own, q_sum)


def exchange(value, axes):
    return lax.all_to_all(value, axes, split_axis=0, concat_axis=0, tiled=True)


def gather(value, axes, parts):
    return exchange(jnp.broadcast_to(value, (parts, *value.shape[1:])), axes)


def on_device(token_ids, activations, grad_out, error_buffer, init_q):
    plane, near = ("x", "y"), ("core", "x", "y")
    parts, peers, depth = lax.axis_size(plane), lax.axis_size(near), lax.axis_size("z")
    replicas = depth * lax.axis_size("core")
    tokens, features = activations.shape
    width = features // parts
    columns = grad_out.shape[1]
    error_rows = error_buffer[0]
    ids = token_ids[None]
    initq_t = init_q.T

    g_all = lax.all_gather(grad_out, plane, axis=0, tiled=True)
    payload = call(
        pack_kernel,
        jax.ShapeDtypeStruct((parts, width + SPLIT_ROWS, tokens), BF16),
        [ANY] * 4,
        ids, activations, grad_out, initq_t,
        scratch=(
            pltpu.VMEM(ids.shape, ids.dtype),
            pltpu.VMEM(activations.shape, BF16),
            pltpu.VMEM(grad_out.shape, BF16),
            pltpu.VMEM(initq_t.shape, F32),
            pltpu.SemaphoreType.DMA((4,)),
        ),
    )
    recv = exchange(payload, plane)
    p_local = call(left_kernel, jax.ShapeDtypeStruct((RANK, width), F32), [VMEM] * 3, recv, error_rows, initq_t)
    p_mean = jnp.sum(gather(lax.psum(p_local, "core")[None], "z", depth), axis=0) / replicas
    p_full = gather(p_mean[None], plane, parts)
    p_own, q_terms = call(
        right_kernel,
        (
            jax.ShapeDtypeStruct((RANK, width), F32),
            jax.ShapeDtypeStruct((columns * RANK // LANES, LANES), F32),
        ),
        [VMEM] * 6,
        p_full, p_mean, ids, activations, grad_out, error_rows,
    )
    blocks = exchange(q_terms.reshape(peers, 1, q_terms.size // peers), near)
    blocks = gather(jnp.sum(blocks, axis=0, keepdims=True), "z", depth)
    q_sum = gather(jnp.sum(blocks, axis=0, keepdims=True), near, peers).reshape(-1, LANES)
    error_next, q_t = final(replicas, recv, g_all, error_rows, p_own, q_sum)
    return p_own.T, q_t.T, error_next[None]


def solution(mesh):
    replicas, parts = mesh.shape["dp"], mesh.shape["fsdp"]
    side = math.isqrt(parts)
    fine = Mesh(mesh.devices.reshape(replicas // 2, 2, side, parts // side), ("z", "core", "x", "y"))
    everywhere = ("z", "core", "x", "y")
    return jax.shard_map(
        on_device,
        mesh=fine,
        in_specs=(
            P(everywhere),
            P(everywhere, None),
            P(everywhere, None),
            P(("z", "core"), ("x", "y"), None),
            P(),
        ),
        out_specs=(P(("x", "y"), None), P(), P(("z", "core"), ("x", "y"), None)),
        check_vma=False,
    )
```

time: 145 us -> 141 us (0.972); the launches traced: 143 us -> 141 us
  Pallas kernels: 13.4 us -> 11.8 us
    psum x2 -> x1, blocking collectives: 14.1 us -> 5.79 us  [on_device(): lax.psum(p_local, 'core')[None]]
    all_to_all x6, blocking collectives: 96.2 us -> 103 us  [exchange(): return lax.all_to_all(value, axes, split_axis=0, concat_axis=0, tiled=True)]
    pallas_call x4, Pallas kernels: 13.4 us -> 11.8 us  [the longest x1 7.57 us: final(): pl.pallas_call(functools.partial(final_kernel, replicas), out_shape=(jax....]
    unnamed x18 -> x16, local copies, waits for them, and re-layouts: 4.26 us -> 4.95 us
  transfers between devices with their start and end apart: 1 -> 1, of which waited for: 0 -> 0; matrix products, arithmetic and copies ran while one was open for 0% -> 0% of each run, Pallas kernels for 2% -> 3%
where the time goes in v2:
time: 141 us
  blocking collectives  109 us (77%)
  between operations  14.1 us (10%)
  Pallas kernels  11.8 us (8%)
  local copies, waits for them, and re-layouts  5.05 us (4%)
    all_to_all x6, blocking collectives, exchange(): return lax.all_to_all(value, axes, split_axis=0, concat_axis=0, tiled=True)  103 us
    pallas_call x1, Pallas kernels, final(): pl.pallas_call(functools.partial(final_kernel, replicas), out_shape=(jax....  7.57 us
    psum x1, blocking collectives, on_device(): lax.psum(p_local, 'core')[None]  5.79 us
    unnamed x16, local copies, waits for them, and re-layouts  4.95 us
    pallas_call x3, Pallas kernels, call(): pl.pallas_call(kernel, out_shape=out_shape, in_specs=specs, out_specs=jax...  4.21 us
  transfers between devices with their start and end apart: 1, of which 0 were waited for; matrix products, arithmetic and copies ran while one was open for 0% of the time, Pallas kernels for 3%

profile of v2, /device:TPU:1, one launch (start us, length us, event | category | flops | bytes accessed | tf_op | source)
XLA Modules:
  0.0 140.8 jit_solution(8227137768497424051)
XLA Ops:
  7.2 0.0 copy-start.1
  7.2 0.0 all-gather.2.cloned.1.call-start
  7.2 0.7 all-gather.2.cloned.1.call-update
  7.9 0.4 copy-done.1
  8.3 0.0 copy-start.2
  8.3 1.1 copy-done.2
  9.4 0.0 copy-start.4
  9.4 0.9 copy-done.4
  10.3 0.0 copy-start.6
  10.3 0.7 copy-done.6
  11.0 1.2 shard_map.76
  12.1 0.0 copy-start
  12.2 20.3 %all_to_all.30.recv_ref = bf16[16,224,128]{2,1,0:T(8,128)(2,1)S(1)} all-to-all(bf16[16,224,128]{2,1,0:T(8,128)(2,1)S(1)} %shard_map.76), channel_id=1, replica_groups=mesh['z'=16,'core'=2,'x'=4,'y'=4] {'x','y'}, dimensions={0} | all-to-all | bytes 1835008 | tf_op jit(solution)/shard_map/all_to_all | solution.py:160
  32.4 0.0 copy-done
  32.4 0.0 copy-start.7
  32.4 0.7 shard_map.77
  33.2 5.8 %psum.7 = f32[8,192]{1,0:T(8,128)S(1)} all-reduce(f32[8,192]{1,0:T(8,128)S(1)} %shard_map.77), channel_id=1, replica_groups=mesh['z'=16,'core'=2,'x'=4,'y'=4] {'core'}, use_global_device_ids=true, to_apply=%region_0.0 | all-reduce | flops 1536 | bytes 12288 | tf_op jit(solution)/shard_map/psum | solution.py:194
  39.0 26.9 %all_to_all.31 = f32[16,8,192]{2,1,0:T(8,128)S(1)} all-to-all(f32[16,8,192]{2,1,0:T(8,128)S(1)} %broadcast_in_dim.13), channel_id=1, replica_groups=mesh['z'=16,'core'=2,'x'=4,'y'=4] {'z'}, dimensions={0} | all-to-all | bytes 196608 | tf_op jit(solution)/shard_map/all_to_all | solution.py:160
  65.9 11.0 %all_to_all.32.pfull_ref = f32[16,8,192]{2,1,0:T(8,128)S(1)} all-to-all(f32[16,8,192]{2,1,0:T(8,128)S(1)} %broadcast_in_dim.14), channel_id=1, replica_groups=mesh['z'=16,'core'=2,'x'=4,'y'=4] {'x','y'}, dimensions={0} | all-to-all | bytes 196608 | tf_op jit(solution)/shard_map/all_to_all | solution.py:160
  76.8 0.0 copy-done.7
  76.8 0.0 copy-start.3
  76.9 1.2 copy-done.3
  78.0 2.3 %shard_map.78 = (f32[8,192]{1,0:T(8,128)}, f32[192,128]{1,0:T(8,128)S(1)}) custom-call(f32[16,8,192]{2,1,0:T(8,128)S(1)} %all_to_all.32.pfull_ref, f32[8,192]{1,0:T(8,128)S(1)} %broadcast_multiply_fusion.pown_ref, s32[1,128]{1,0:T(1,128)S(1)} %bitcast.17, bf16[128,3072]{1,0:T(8,128)(2,1)S(1)} %copy-done.3, bf16[128,3072]{1,0:T(8,128)(2,1)S(1)} %copy-done.1, ...), custom_call_target="tpu_custom_call" | custom-call | bytes 2857472 | tf_op jit(solution)/shard_map/pallas_call | solution.py:55
  80.4 16.6 %all_to_all.33 = f32[32,1,768]{2,1,0:T(1,128)S(1)} all-to-all(f32[32,1,768]{2,1,0:T(1,128)S(1)} %bitcast.14), channel_id=1, replica_groups=mesh['z'=16,'core'=2,'x'=4,'y'=4] {'core','x','y'}, dimensions={0} | all-to-all | bytes 196608 | tf_op jit(solution)/shard_map/all_to_all | solution.py:160
  96.9 0.1 reduce_sum.28
  97.0 15.2 %all_to_all.34 = f32[16,1,768]{2,1,0:T(1,128)S(1)} all-to-all(f32[16,1,768]{2,1,0:T(1,128)S(1)} %broadcast_in_dim.15), channel_id=1, replica_groups=mesh['z'=16,'core'=2,'x'=4,'y'=4] {'z'}, dimensions={0} | all-to-all | bytes 98304 | tf_op jit(solution)/shard_map/all_to_all | solution.py:160
  112.3 0.1 broadcast_in_dim.16
  112.3 13.4 %all_to_all.35 = f32[32,1,768]{2,1,0:T(1,128)S(1)} all-to-all(f32[32,1,768]{2,1,0:T(1,128)S(1)} %broadcast_in_dim.16), channel_id=1, replica_groups=mesh['z'=16,'core'=2,'x'=4,'y'=4] {'core','x','y'}, dimensions={0} | all-to-all | bytes 196608 | tf_op jit(solution)/shard_map/all_to_all | solution.py:160
  125.7 0.0 all-gather.2.cloned.1.call-done.g_ref
  125.7 0.0 copy-start.5
  125.7 0.7 copy-done.5
  126.4 7.6 %shard_map.79 = (bf16[192,3072]{1,0:T(8,128)(2,1)}, f32[8,3072]{1,0:T(8,128)}) custom-call(bf16[16,224,128]{2,1,0:T(8,128)(2,1)S(1)} %all_to_all.30.recv_ref, bf16[2048,3072]{1,0:T(8,128)(2,1)} %all-gather.2.cloned.1.call-done.g_ref, bf16[192,3072]{1,0:T(8,128)(2,1)S(1)} %bitcast.10, f32[8,192]{1,0:T(8,128)S(1)} %copy-done.5, f32[192,128]{1,0:T(8,128)S(1)} %bitcast.11), custom_call_target="tpu_custom_call" | custom-call | flops 2415919104 | bytes 14942208 | tf_op jit(solution)/shard_map/pallas_call | solution.py:138
  (6 shorter events, 0.1 us)
Async XLA Ops:
  7.2 1.1 copy-start.1
  7.2 118.5 %all-gather.2.cloned.1.call-start = ((), (), s32[]{:S(2)}) async-start(), calls=%async_computation.6 | async-start | bytes 13369344 | tf_op jit(solution)/shard_map/all_gather | solution.py:178
  8.3 1.1 copy-start.2
  9.4 0.9 copy-start.4
  10.3 0.7 copy-start.6
  12.1 20.3 %copy-start = (bf16[1,192,3072]{2,1,0:T(8,128)(2,1)S(1)}, bf16[1,192,3072]{2,1,0:T(8,128)(2,1)}, u32[]{:S(2)}) copy-start(bf16[1,192,3072]{2,1,0:T(8,128)(2,1)} %param.8) | copy-start | bytes 3538948
  32.4 44.4 %copy-start.7 = (s32[128]{0:T(128)S(1)}, s32[128]{0:T(128)}, u32[]{:S(2)}) copy-start(s32[128]{0:T(128)} %param.5) | copy-start | bytes 1540
  76.8 1.2 copy-start.3
  125.7 0.7 copy-start.5
Sparse Core Ops, SparseCore 0:
  11.1 114.0 all-gather.1

commit v3 on v2

--- a/solution.py
+++ b/solution.py
@@ -10,13 +10,14 @@
 
 RANK = 8
 LANES = 128
-SPLIT_ROWS = 4 * RANK
+SPLIT_ROWS = 2 * RANK
 F32, BF16 = jnp.float32, jnp.bfloat16
 NT = (((1,), (1,)), ((), ()))
 TN = (((0,), (0,)), ((), ()))
 XP_SCALE = 2.0**-8
+TOKEN_CUTS, COLUMN_CUTS = 8, 2
 VMEM = pl.BlockSpec(memory_space=pltpu.VMEM)
-ANY = pl.BlockSpec(memory_space=pl.ANY)
+HBM = pl.BlockSpec(memory_space=pltpu.HBM)
 
 
 def terms(value):
@@ -50,7 +51,11 @@
     return jnp.concatenate([ref[i, rows, :] for i in range(ref.shape[0])], axis=1)
 
 
-def call(kernel, out_shape, specs, *args, scratch=(), flops=0):
+def staged(*arrays):
+    return [pltpu.VMEM(a.shape, a.dtype) for a in arrays]
+
+
+def call(kernel, out_shape, specs, *args, scratch=(), vmem=40):
     nbytes = sum(math.prod(a.shape) * a.dtype.itemsize for a in args)
     return pl.pallas_call(
         kernel,
@@ -58,8 +63,8 @@
         in_specs=specs,
         out_specs=jax.tree.map(lambda _: VMEM, out_shape),
         scratch_shapes=scratch,
-        compiler_params=pltpu.CompilerParams(vmem_limit_bytes=40 * 2**20),
-        cost_estimate=pl.CostEstimate(flops=flops, bytes_accessed=nbytes, transcendentals=0),
+        compiler_params=pltpu.CompilerParams(vmem_limit_bytes=vmem * 2**20),
+        cost_estimate=pl.CostEstimate(flops=0, bytes_accessed=nbytes, transcendentals=0),
     )(*args)
 
 
@@ -74,7 +79,8 @@
     parts, rows, _ = pay_ref.shape
     width = rows - SPLIT_ROWS
     valid = (ids_ref[...] != 1).astype(F32)
-    gq = split(join(dot(split(initq_ref[...]), g_ref[...], NT)) * valid)
+    gq = join(dot(split(initq_ref[...]), g_ref[...], NT)) * valid
+    gq = jnp.concatenate(terms(gq)[:2], axis=0).astype(BF16)
     copies[3].wait()
     for i in range(parts):
         block = x_ref[:, i * width : (i + 1) * width].astype(F32).T * valid
@@ -86,7 +92,8 @@
     width = recv_ref.shape[1] - SPLIT_ROWS
     x_cols = lanes(recv_ref, slice(0, width))
     gq = lanes(recv_ref, slice(width, None))
-    p_ref[...] = join(dot(gq, x_cols, NT)) + join(dot(split(initq_ref[...]), e_ref[...], NT))
+    p = dot(gq, x_cols, NT)
+    p_ref[...] = p[:RANK] + p[RANK:] + join(dot(split(initq_ref[...]), e_ref[...], NT))
 
 
 def inverse_factor(gram):
@@ -104,7 +111,13 @@
     return right * scale
 
 
-def right_kernel(pfull_ref, pown_ref, ids_ref, x_ref, g_ref, e_ref, own_ref, q_ref):
+def right_kernel(
+    pfull_ref, pown_ref, ids_hbm, x_hbm, g_hbm, e_ref, own_ref, again_ref, q_ref, ids_ref, x_ref, g_ref, sems
+):
+    pairs = ((ids_hbm, ids_ref), (x_hbm, x_ref), (g_hbm, g_ref))
+    copies = [pltpu.make_async_copy(*pair, sems.at[i]) for i, pair in enumerate(pairs)]
+    for copy in copies:
+        copy.start()
     high = dict(precision=lax.Precision.HIGHEST, preferred_element_type=F32)
     p_full = lanes(pfull_ref)
     gram = lax.dot_general(p_full, p_full, NT, **high)
@@ -112,6 +125,9 @@
     factor = jnp.dot(inverse, p_full, **high)
     own = jnp.dot(inverse, pown_ref[...], **high)
     own_ref[...] = own
+    again_ref[...] = own
+    for copy in copies:
+        copy.wait()
     valid = ids_ref[...] != 1
     xp = join(dot(split(factor * XP_SCALE), x_ref[...], NT))
     xp = split(jnp.where(valid, xp, 0.0))
@@ -119,38 +135,58 @@
     q_ref[...] = stack(q)
 
 
-def final_kernel(replicas, recv_ref, g_ref, e_ref, p_ref, q_ref, out_ref, qout_ref):
-    width = out_ref.shape[0]
+def final_kernel(
+    replicas, recv_ref, g_hbm, e_ref, p_ref, q_ref, out_hbm, qout_ref, g_ref, total_ref, out_ref, in_sems, out_sems
+):
+    width, columns = e_ref.shape
+    rows, wide = g_hbm.shape[0] // TOKEN_CUTS, columns // COLUMN_CUTS
+    spans = [slice(i, i + rows) for i in range(0, g_hbm.shape[0], rows)]
+    sides = [slice(j, j + wide) for j in range(0, columns, wide)]
+    loads = [pltpu.make_async_copy(g_hbm.at[s], g_ref.at[s], in_sems.at[i]) for i, s in enumerate(spans)]
+    stores = [pltpu.make_async_copy(out_ref.at[:, s], out_hbm.at[:, s], out_sems.at[j]) for j, s in enumerate(sides)]
+    for load in loads:
+        load.start()
     q = unstack(q_ref[...]) * (1.0 / replicas)
     qout_ref[...] = q
     p_high, p_middle, p_low = terms(p_ref[...])
     q_high, q_middle, q_low = terms(q)
     p_terms = jnp.concatenate([p_high, p_high, p_middle, p_high, p_low, p_middle], axis=0).astype(BF16)
     q_terms = jnp.concatenate([q_high, q_middle, q_high, q_low, q_high, q_middle], axis=0).astype(BF16)
-    merged = dot(lanes(recv_ref, slice(0, width)), g_ref[...]) + e_ref[...].astype(F32)
-    out_ref[...] = (merged - dot(p_terms, q_terms, TN)).astype(BF16)
+    for side in sides:
+        total_ref[:, side] = e_ref[:, side].astype(F32) - dot(p_terms, q_terms[:, side], TN)
+    x_cols = lanes(recv_ref, slice(0, width))
+    for i, span in enumerate(spans):
+        loads[i].wait()
+        for j, side in enumerate(sides):
+            total = total_ref[:, side] + dot(x_cols[:, span], g_ref[span, side])
+            if i + 1 < len(spans):
+                total_ref[:, side] = total
+            else:
+                out_ref[:, side] = total.astype(BF16)
+                stores[j].start()
+    for store in stores:
+        store.wait()
 
 
 def final(replicas, recv, g_all, error_rows, p_own, q_sum):
-    parts, _, tokens = recv.shape
     width, columns = error_rows.shape
-    tile = math.gcd(columns, 768)
+    outs = (jax.ShapeDtypeStruct((width, columns), BF16), jax.ShapeDtypeStruct((RANK, columns), F32))
     return pl.pallas_call(
         functools.partial(final_kernel, replicas),
-        out_shape=(jax.ShapeDtypeStruct((width, columns), BF16), jax.ShapeDtypeStruct((RANK, columns), F32)),
-        grid=(columns // tile,),
-        in_specs=[
-            pl.BlockSpec(recv.shape, lambda j: (0, 0, 0)),
-            pl.BlockSpec((parts * tokens, tile), lambda j: (0, j)),
-            pl.BlockSpec((width, tile), lambda j: (0, j)),
-            pl.BlockSpec((RANK, width), lambda j: (0, 0)),
-            pl.BlockSpec((tile * RANK // LANES, LANES), lambda j: (j, 0)),
-        ],
-        out_specs=(pl.BlockSpec((width, tile), lambda j: (0, j)), pl.BlockSpec((RANK, tile), lambda j: (0, j))),
-        compiler_params=pltpu.CompilerParams(vmem_limit_bytes=40 * 2**20),
+        out_shape=outs,
+        in_specs=[VMEM, HBM, VMEM, VMEM, VMEM],
+        out_specs=(HBM, VMEM),
+        scratch_shapes=(
+            *staged(g_all),
+            pltpu.VMEM(error_rows.shape, F32),
+            *staged(error_rows),
+            pltpu.SemaphoreType.DMA((TOKEN_CUTS,)),
+            pltpu.SemaphoreType.DMA((COLUMN_CUTS,)),
+        ),
+        compiler_params=pltpu.CompilerParams(vmem_limit_bytes=48 * 2**20),
         cost_estimate=pl.CostEstimate(
-            flops=2 * width * columns * parts * tokens,
-            bytes_accessed=2 * columns * (parts * tokens + 2 * width),
+            flops=2 * width * columns * g_all.shape[0],
+            bytes_accessed=2 * columns * (g_all.shape[0] + 2 * width),
             transcendentals=0,
         ),
     )(recv, g_all, error_rows, p_own, q_sum)
@@ -179,33 +215,30 @@
     payload = call(
         pack_kernel,
         jax.ShapeDtypeStruct((parts, width + SPLIT_ROWS, tokens), BF16),
-        [ANY] * 4,
+        [HBM] * 4,
         ids, activations, grad_out, initq_t,
-        scratch=(
-            pltpu.VMEM(ids.shape, ids.dtype),
-            pltpu.VMEM(activations.shape, BF16),
-            pltpu.VMEM(grad_out.shape, BF16),
-            pltpu.VMEM(initq_t.shape, F32),
-            pltpu.SemaphoreType.DMA((4,)),
-        ),
+        scratch=(*staged(ids, activations, grad_out, initq_t), pltpu.SemaphoreType.DMA((4,))),
+        vmem=62,
     )
     recv = exchange(payload, plane)
     p_local = call(left_kernel, jax.ShapeDtypeStruct((RANK, width), F32), [VMEM] * 3, recv, error_rows, initq_t)
     p_mean = jnp.sum(gather(lax.psum(p_local, "core")[None], "z", depth), axis=0) / replicas
     p_full = gather(p_mean[None], plane, parts)
-    p_own, q_terms = call(
+    p_own, p_again, q_terms = call(
         right_kernel,
         (
             jax.ShapeDtypeStruct((RANK, width), F32),
+            jax.ShapeDtypeStruct((RANK, width), F32),
             jax.ShapeDtypeStruct((columns * RANK // LANES, LANES), F32),
         ),
-        [VMEM] * 6,
+        [VMEM, VMEM, HBM, HBM, HBM, VMEM],
         p_full, p_mean, ids, activations, grad_out, error_rows,
+        scratch=(*staged(ids, activations, grad_out), pltpu.SemaphoreType.DMA((3,))),
     )
     blocks = exchange(q_terms.reshape(peers, 1, q_terms.size // peers), near)
     blocks = gather(jnp.sum(blocks, axis=0, keepdims=True), "z", depth)
     q_sum = gather(jnp.sum(blocks, axis=0, keepdims=True), near, peers).reshape(-1, LANES)
-    error_next, q_t = final(replicas, recv, g_all, error_rows, p_own, q_sum)
+    error_next, q_t = final(replicas, recv, g_all, error_rows, p_again, q_sum)
     return p_own.T, q_t.T, error_next[None]
 
 

time: 141 us -> 139 us (0.986)
  local copies, waits for them, and re-layouts: 5.05 us -> 1.26 us
    unnamed x16 -> x10, local copies, waits for them, and re-layouts: 4.95 us -> 1.15 us
    pallas_call x3, Pallas kernels: 4.21 us -> 6.49 us  [call(): pl.pallas_call(kernel, out_shape=out_shape, in_specs=specs, out_specs=jax...]
  transfers between devices with their start and end apart: 1 -> 1, of which waited for: 0 -> 1; matrix products, arithmetic and copies ran while one was open for 0% -> 0% of each run, Pallas kernels for 3% -> 5%
where the time goes in v3:
time: 139 us
  blocking collectives  109 us (78%)
  between operations  14.1 us (10%)
  Pallas kernels  13.2 us (9%)
  waiting for transfers between devices  1.41 us (1%)
    all_to_all x6, blocking collectives, exchange(): return lax.all_to_all(value, axes, split_axis=0, concat_axis=0, tiled=True)  102 us
    pallas_call x1, Pallas kernels, final(): pl.pallas_call(functools.partial(final_kernel, replicas), out_shape=outs,...  6.7 us
    psum x1, blocking collectives, on_device(): lax.psum(p_local, 'core')[None]  6.59 us
    pallas_call x3, Pallas kernels, call(): pl.pallas_call(kernel, out_shape=out_shape, in_specs=specs, out_specs=jax...  6.49 us
  transfers between devices with their start and end apart: 1, of which 1 were waited for; matrix products, arithmetic and copies ran while one was open for 0% of the time, Pallas kernels for 5%

profile of v3, /device:TPU:1, one launch (start us, length us, event | category | flops | bytes accessed | tf_op | source)
XLA Modules:
  0.0 138.7 jit_solution(4030392998245108436)
XLA Ops:
  7.2 0.0 all-gather.2.cloned.1.call-start
  7.2 0.7 all-gather.2.cloned.1.call-update
  7.9 3.0 %shard_map.76 = bf16[16,208,128]{2,1,0:T(8,128)(2,1)} custom-call(s32[1,128]{1,0:T(1,128)} %bitcast.15, bf16[128,3072]{1,0:T(8,128)(2,1)} %x_hbm.3, bf16[128,3072]{1,0:T(8,128)(2,1)} %g_hbm.3, f32[8,3072]{1,0:T(8,128)} %bitcast.12), custom_call_target="tpu_custom_call" | custom-call | bytes 1671680 | tf_op jit(solution)/shard_map/pallas_call | solution.py:60
  11.0 0.0 copy-start
  11.0 0.0 copy-start.3
  11.0 19.0 %all_to_all.30.recv_ref = bf16[16,208,128]{2,1,0:T(8,128)(2,1)S(1)} all-to-all(bf16[16,208,128]{2,1,0:T(8,128)(2,1)} %shard_map.76), channel_id=1, replica_groups=mesh['z'=16,'core'=2,'x'=4,'y'=4] {'x','y'}, dimensions={0} | all-to-all | bytes 1703936 | tf_op jit(solution)/shard_map/all_to_all | solution.py:196
  30.0 0.0 copy-done
  30.0 0.0 copy-done.3
  30.0 0.0 copy-start.1
  30.0 0.0 copy-start.4
  30.0 0.6 shard_map.77
  30.7 6.6 %psum.7 = f32[8,192]{1,0:T(8,128)S(1)} all-reduce(f32[8,192]{1,0:T(8,128)S(1)} %shard_map.77), channel_id=1, replica_groups=mesh['z'=16,'core'=2,'x'=4,'y'=4] {'core'}, use_global_device_ids=true, to_apply=%region_0.0 | all-reduce | flops 1536 | bytes 12288 | tf_op jit(solution)/shard_map/psum | solution.py:225
  37.3 26.9 %all_to_all.31 = f32[16,8,192]{2,1,0:T(8,128)S(1)} all-to-all(f32[16,8,192]{2,1,0:T(8,128)S(1)} %broadcast_in_dim.13), channel_id=1, replica_groups=mesh['z'=16,'core'=2,'x'=4,'y'=4] {'z'}, dimensions={0} | all-to-all | bytes 196608 | tf_op jit(solution)/shard_map/all_to_all | solution.py:196
  64.2 10.7 %all_to_all.32.pfull_ref = f32[16,8,192]{2,1,0:T(8,128)S(1)} all-to-all(f32[16,8,192]{2,1,0:T(8,128)S(1)} %broadcast_in_dim.14), channel_id=1, replica_groups=mesh['z'=16,'core'=2,'x'=4,'y'=4] {'x','y'}, dimensions={0} | all-to-all | bytes 196608 | tf_op jit(solution)/shard_map/all_to_all | solution.py:196
  74.8 0.0 copy-done.1
  74.9 0.0 copy-done.4
  74.9 0.0 copy-start.2
  74.9 1.1 copy-done.2
  76.0 2.8 %shard_map.78 = (f32[8,192]{1,0:T(8,128)}, f32[8,192]{1,0:T(8,128)S(1)}, f32[192,128]{1,0:T(8,128)S(1)}) custom-call(f32[16,8,192]{2,1,0:T(8,128)S(1)} %all_to_all.32.pfull_ref, f32[8,192]{1,0:T(8,128)S(1)} %broadcast_multiply_fusion.pown_ref, s32[1,128]{1,0:T(1,128)S(1)} %bitcast.16, bf16[128,3072]{1,0:T(8,128)(2,1)S(1)} %copy-done.2, ...), custom_call_target="tpu_custom_call" | custom-call | bytes 2857472 | tf_op jit(solution)/shard_map/pallas_call | solution.py:60
  78.8 16.9 %all_to_all.33 = f32[32,1,768]{2,1,0:T(1,128)S(1)} all-to-all(f32[32,1,768]{2,1,0:T(1,128)S(1)} %bitcast.14), channel_id=1, replica_groups=mesh['z'=16,'core'=2,'x'=4,'y'=4] {'core','x','y'}, dimensions={0} | all-to-all | bytes 196608 | tf_op jit(solution)/shard_map/all_to_all | solution.py:196
  95.7 0.1 reduce_sum.28
  95.8 15.1 %all_to_all.34 = f32[16,1,768]{2,1,0:T(1,128)S(1)} all-to-all(f32[16,1,768]{2,1,0:T(1,128)S(1)} %broadcast_in_dim.15), channel_id=1, replica_groups=mesh['z'=16,'core'=2,'x'=4,'y'=4] {'z'}, dimensions={0} | all-to-all | bytes 98304 | tf_op jit(solution)/shard_map/all_to_all | solution.py:196
  111.0 0.1 broadcast_in_dim.16
  111.0 13.4 %all_to_all.35 = f32[32,1,768]{2,1,0:T(1,128)S(1)} all-to-all(f32[32,1,768]{2,1,0:T(1,128)S(1)} %broadcast_in_dim.16), channel_id=1, replica_groups=mesh['z'=16,'core'=2,'x'=4,'y'=4] {'core','x','y'}, dimensions={0} | all-to-all | bytes 196608 | tf_op jit(solution)/shard_map/all_to_all | solution.py:196
  124.4 0.7 all-gather.2.cloned.1.call-done.g_hbm
  125.2 6.7 %shard_map.79 = (bf16[192,3072]{1,0:T(8,128)(2,1)}, f32[8,3072]{1,0:T(8,128)}) custom-call(bf16[16,208,128]{2,1,0:T(8,128)(2,1)S(1)} %all_to_all.30.recv_ref, bf16[2048,3072]{1,0:T(8,128)(2,1)} %all-gather.2.cloned.1.call-done.g_hbm, bf16[192,3072]{1,0:T(8,128)(2,1)S(1)} %bitcast.10, f32[8,192]{1,0:T(8,128)S(1)} %get-tuple-element.9.p_ref, ...), custom_call_target="tpu_custom_call" | custom-call | flops 2415919104 | bytes 14942208 | tf_op jit(solution)/shard_map/pallas_call | solution.py:174
  (6 shorter events, 0.1 us)
Async XLA Ops:
  7.2 118.0 %all-gather.2.cloned.1.call-start = ((), (), s32[]{:S(2)}) async-start(), calls=%async_computation.6 | async-start | bytes 13369344 | tf_op jit(solution)/shard_map/all_gather | solution.py:214
  11.0 19.1 %copy-start = (bf16[1,192,3072]{2,1,0:T(8,128)(2,1)S(1)}, bf16[1,192,3072]{2,1,0:T(8,128)(2,1)}, u32[]{:S(2)}) copy-start(bf16[1,192,3072]{2,1,0:T(8,128)(2,1)} %param.8) | copy-start | bytes 3538948
  11.0 19.0 %copy-start.3 = (f32[3072,8]{0,1:T(8,128)S(1)}, f32[3072,8]{0,1:T(8,128)}, u32[]{:S(2)}) copy-start(f32[3072,8]{0,1:T(8,128)} %param.9) | copy-start | bytes 294916
  30.0 44.8 %copy-start.1 = (bf16[128,3072]{1,0:T(8,128)(2,1)S(1)}, bf16[128,3072]{1,0:T(8,128)(2,1)}, u32[]{:S(2)}) copy-start(bf16[128,3072]{1,0:T(8,128)(2,1)} %g_hbm.3) | copy-start | bytes 2359300
  30.0 44.8 %copy-start.4 = (s32[128]{0:T(128)S(1)}, s32[128]{0:T(128)}, u32[]{:S(2)}) copy-start(s32[128]{0:T(128)} %param.5) | copy-start | bytes 1540
  74.9 1.1 copy-start.2
Sparse Core Ops, SparseCore 0:
  11.1 114.0 all-gather.1

commit v4 on v3

--- a/solution.py
+++ b/solution.py
@@ -15,7 +15,8 @@
 NT = (((1,), (1,)), ((), ()))
 TN = (((0,), (0,)), ((), ()))
 XP_SCALE = 2.0**-8
-TOKEN_CUTS, COLUMN_CUTS = 8, 2
+TOKEN_CUTS = (0, 1, 3, 5, 7, 8)
+COLUMN_CUTS = 2
 VMEM = pl.BlockSpec(memory_space=pltpu.VMEM)
 HBM = pl.BlockSpec(memory_space=pltpu.HBM)
 
@@ -139,8 +140,9 @@
     replicas, recv_ref, g_hbm, e_ref, p_ref, q_ref, out_hbm, qout_ref, g_ref, total_ref, out_ref, in_sems, out_sems
 ):
     width, columns = e_ref.shape
-    rows, wide = g_hbm.shape[0] // TOKEN_CUTS, columns // COLUMN_CUTS
-    spans = [slice(i, i + rows) for i in range(0, g_hbm.shape[0], rows)]
+    wide = columns // COLUMN_CUTS
+    cuts = [g_hbm.shape[0] * eighths // 8 for eighths in TOKEN_CUTS]
+    spans = [slice(*pair) for pair in zip(cuts, cuts[1:])]
     sides = [slice(j, j + wide) for j in range(0, columns, wide)]
     loads = [pltpu.make_async_copy(g_hbm.at[s], g_ref.at[s], in_sems.at[i]) for i, s in enumerate(spans)]
     stores = [pltpu.make_async_copy(out_ref.at[:, s], out_hbm.at[:, s], out_sems.at[j]) for j, s in enumerate(sides)]
@@ -180,7 +182,7 @@
             *staged(g_all),
             pltpu.VMEM(error_rows.shape, F32),
             *staged(error_rows),
-            pltpu.SemaphoreType.DMA((TOKEN_CUTS,)),
+            pltpu.SemaphoreType.DMA((len(TOKEN_CUTS) - 1,)),
             pltpu.SemaphoreType.DMA((COLUMN_CUTS,)),
         ),
         compiler_params=pltpu.CompilerParams(vmem_limit_bytes=48 * 2**20),

time: 139 us -> 140 us (level)
  no operation moved by 1% of the time
where the time goes in v4:
time: 140 us; the launch traced here: 139 us
  blocking collectives  109 us (78%)
  between operations  14.1 us (10%)
  Pallas kernels  13.6 us (10%)
  waiting for transfers between devices  1.41 us (1%)
    all_to_all x6, blocking collectives, exchange(): return lax.all_to_all(value, axes, split_axis=0, concat_axis=0, tiled=True)  102 us
    pallas_call x1, Pallas kernels, final(): pl.pallas_call(functools.partial(final_kernel, replicas), out_shape=outs,...  7.08 us
    psum x1, blocking collectives, on_device(): lax.psum(p_local, 'core')[None]  6.59 us
    pallas_call x3, Pallas kernels, call(): pl.pallas_call(kernel, out_shape=out_shape, in_specs=specs, out_specs=jax...  6.49 us
  transfers between devices with their start and end apart: 1, of which 1 were waited for; matrix products, arithmetic and copies ran while one was open for 0% of the time, Pallas kernels for 5%

profile of v4, /device:TPU:1, one launch (start us, length us, event | category | flops | bytes accessed | tf_op | source)
XLA Modules:
  0.0 139.1 jit_solution(9891919247445414299)
XLA Ops:
  7.2 0.0 all-gather.2.cloned.1.call-start
  7.2 0.7 all-gather.2.cloned.1.call-update
  7.9 3.0 %shard_map.76 = bf16[16,208,128]{2,1,0:T(8,128)(2,1)} custom-call(s32[1,128]{1,0:T(1,128)} %bitcast.15, bf16[128,3072]{1,0:T(8,128)(2,1)} %x_hbm.3, bf16[128,3072]{1,0:T(8,128)(2,1)} %g_hbm.3, f32[8,3072]{1,0:T(8,128)} %bitcast.12), custom_call_target="tpu_custom_call" | custom-call | bytes 1671680 | tf_op jit(solution)/shard_map/pallas_call | solution.py:61
  11.0 0.0 copy-start
  11.0 0.0 copy-start.3
  11.0 19.0 %all_to_all.30.recv_ref = bf16[16,208,128]{2,1,0:T(8,128)(2,1)S(1)} all-to-all(bf16[16,208,128]{2,1,0:T(8,128)(2,1)} %shard_map.76), channel_id=1, replica_groups=mesh['z'=16,'core'=2,'x'=4,'y'=4] {'x','y'}, dimensions={0} | all-to-all | bytes 1703936 | tf_op jit(solution)/shard_map/all_to_all | solution.py:198
  30.0 0.0 copy-done
  30.0 0.0 copy-done.3
  30.0 0.0 copy-start.1
  30.0 0.0 copy-start.4
  30.0 0.6 shard_map.77
  30.7 6.6 %psum.7 = f32[8,192]{1,0:T(8,128)S(1)} all-reduce(f32[8,192]{1,0:T(8,128)S(1)} %shard_map.77), channel_id=1, replica_groups=mesh['z'=16,'core'=2,'x'=4,'y'=4] {'core'}, use_global_device_ids=true, to_apply=%region_0.0 | all-reduce | flops 1536 | bytes 12288 | tf_op jit(solution)/shard_map/psum | solution.py:227
  37.3 26.9 %all_to_all.31 = f32[16,8,192]{2,1,0:T(8,128)S(1)} all-to-all(f32[16,8,192]{2,1,0:T(8,128)S(1)} %broadcast_in_dim.13), channel_id=1, replica_groups=mesh['z'=16,'core'=2,'x'=4,'y'=4] {'z'}, dimensions={0} | all-to-all | bytes 196608 | tf_op jit(solution)/shard_map/all_to_all | solution.py:198
  64.2 10.7 %all_to_all.32.pfull_ref = f32[16,8,192]{2,1,0:T(8,128)S(1)} all-to-all(f32[16,8,192]{2,1,0:T(8,128)S(1)} %broadcast_in_dim.14), channel_id=1, replica_groups=mesh['z'=16,'core'=2,'x'=4,'y'=4] {'x','y'}, dimensions={0} | all-to-all | bytes 196608 | tf_op jit(solution)/shard_map/all_to_all | solution.py:198
  74.8 0.0 copy-done.1
  74.9 0.0 copy-done.4
  74.9 0.0 copy-start.2
  74.9 1.1 copy-done.2
  76.0 2.8 %shard_map.78 = (f32[8,192]{1,0:T(8,128)}, f32[8,192]{1,0:T(8,128)S(1)}, f32[192,128]{1,0:T(8,128)S(1)}) custom-call(f32[16,8,192]{2,1,0:T(8,128)S(1)} %all_to_all.32.pfull_ref, f32[8,192]{1,0:T(8,128)S(1)} %broadcast_multiply_fusion.pown_ref, s32[1,128]{1,0:T(1,128)S(1)} %bitcast.16, bf16[128,3072]{1,0:T(8,128)(2,1)S(1)} %copy-done.2, ...), custom_call_target="tpu_custom_call" | custom-call | bytes 2857472 | tf_op jit(solution)/shard_map/pallas_call | solution.py:61
  78.8 16.9 %all_to_all.33 = f32[32,1,768]{2,1,0:T(1,128)S(1)} all-to-all(f32[32,1,768]{2,1,0:T(1,128)S(1)} %bitcast.14), channel_id=1, replica_groups=mesh['z'=16,'core'=2,'x'=4,'y'=4] {'core','x','y'}, dimensions={0} | all-to-all | bytes 196608 | tf_op jit(solution)/shard_map/all_to_all | solution.py:198
  95.7 0.1 reduce_sum.28
  95.8 15.1 %all_to_all.34 = f32[16,1,768]{2,1,0:T(1,128)S(1)} all-to-all(f32[16,1,768]{2,1,0:T(1,128)S(1)} %broadcast_in_dim.15), channel_id=1, replica_groups=mesh['z'=16,'core'=2,'x'=4,'y'=4] {'z'}, dimensions={0} | all-to-all | bytes 98304 | tf_op jit(solution)/shard_map/all_to_all | solution.py:198
  111.0 0.1 broadcast_in_dim.16
  111.0 13.4 %all_to_all.35 = f32[32,1,768]{2,1,0:T(1,128)S(1)} all-to-all(f32[32,1,768]{2,1,0:T(1,128)S(1)} %broadcast_in_dim.16), channel_id=1, replica_groups=mesh['z'=16,'core'=2,'x'=4,'y'=4] {'core','x','y'}, dimensions={0} | all-to-all | bytes 196608 | tf_op jit(solution)/shard_map/all_to_all | solution.py:198
  124.4 0.7 all-gather.2.cloned.1.call-done.g_hbm
  125.2 7.1 %shard_map.79 = (bf16[192,3072]{1,0:T(8,128)(2,1)}, f32[8,3072]{1,0:T(8,128)}) custom-call(bf16[16,208,128]{2,1,0:T(8,128)(2,1)S(1)} %all_to_all.30.recv_ref, bf16[2048,3072]{1,0:T(8,128)(2,1)} %all-gather.2.cloned.1.call-done.g_hbm, bf16[192,3072]{1,0:T(8,128)(2,1)S(1)} %bitcast.10, f32[8,192]{1,0:T(8,128)S(1)} %get-tuple-element.9.p_ref, ...), custom_call_target="tpu_custom_call" | custom-call | flops 2415919104 | bytes 14942208 | tf_op jit(solution)/shard_map/pallas_call | solution.py:176
  (6 shorter events, 0.1 us)
Async XLA Ops:
  7.2 118.0 %all-gather.2.cloned.1.call-start = ((), (), s32[]{:S(2)}) async-start(), calls=%async_computation.6 | async-start | bytes 13369344 | tf_op jit(solution)/shard_map/all_gather | solution.py:216
  11.0 19.1 %copy-start = (bf16[1,192,3072]{2,1,0:T(8,128)(2,1)S(1)}, bf16[1,192,3072]{2,1,0:T(8,128)(2,1)}, u32[]{:S(2)}) copy-start(bf16[1,192,3072]{2,1,0:T(8,128)(2,1)} %param.8) | copy-start | bytes 3538948
  11.0 19.0 %copy-start.3 = (f32[3072,8]{0,1:T(8,128)S(1)}, f32[3072,8]{0,1:T(8,128)}, u32[]{:S(2)}) copy-start(f32[3072,8]{0,1:T(8,128)} %param.9) | copy-start | bytes 294916
  30.0 44.8 %copy-start.1 = (bf16[128,3072]{1,0:T(8,128)(2,1)S(1)}, bf16[128,3072]{1,0:T(8,128)(2,1)}, u32[]{:S(2)}) copy-start(bf16[128,3072]{1,0:T(8,128)(2,1)} %g_hbm.3) | copy-start | bytes 2359300
  30.0 44.8 %copy-start.4 = (s32[128]{0:T(128)S(1)}, s32[128]{0:T(128)}, u32[]{:S(2)}) copy-start(s32[128]{0:T(128)} %param.5) | copy-start | bytes 1540
  74.9 1.1 copy-start.2
Sparse Core Ops, SparseCore 0:
  11.1 114.0 all-gather.1

commit v5 on v4

--- a/solution.py
+++ b/solution.py
@@ -15,7 +15,7 @@
 NT = (((1,), (1,)), ((), ()))
 TN = (((0,), (0,)), ((), ()))
 XP_SCALE = 2.0**-8
-TOKEN_CUTS = (0, 1, 3, 5, 7, 8)
+TOKEN_CUTS = (0, 1, 2, 4, 6, 8, 10, 12, 14, 15, 16)
 COLUMN_CUTS = 2
 VMEM = pl.BlockSpec(memory_space=pltpu.VMEM)
 HBM = pl.BlockSpec(memory_space=pltpu.HBM)
@@ -141,7 +141,7 @@
 ):
     width, columns = e_ref.shape
     wide = columns // COLUMN_CUTS
-    cuts = [g_hbm.shape[0] * eighths // 8 for eighths in TOKEN_CUTS]
+    cuts = [g_hbm.shape[0] * part // 16 for part in TOKEN_CUTS]
     spans = [slice(*pair) for pair in zip(cuts, cuts[1:])]
     sides = [slice(j, j + wide) for j in range(0, columns, wide)]
     loads = [pltpu.make_async_copy(g_hbm.at[s], g_ref.at[s], in_sems.at[i]) for i, s in enumerate(spans)]

time: 140 us -> 140 us (level)
  no operation moved by 1% of the time
where the time goes in v5:
time: 140 us; the launch traced here: 139 us
  blocking collectives  109 us (78%)
  between operations  14.1 us (10%)
  Pallas kernels  13.5 us (10%)
  waiting for transfers between devices  1.41 us (1%)
    all_to_all x6, blocking collectives, exchange(): return lax.all_to_all(value, axes, split_axis=0, concat_axis=0, tiled=True)  102 us
    pallas_call x1, Pallas kernels, final(): pl.pallas_call(functools.partial(final_kernel, replicas), out_shape=outs,...  7.03 us
    psum x1, blocking collectives, on_device(): lax.psum(p_local, 'core')[None]  6.59 us
    pallas_call x3, Pallas kernels, call(): pl.pallas_call(kernel, out_shape=out_shape, in_specs=specs, out_specs=jax...  6.49 us
  transfers between devices with their start and end apart: 1, of which 1 were waited for; matrix products, arithmetic and copies ran while one was open for 0% of the time, Pallas kernels for 5%

profile of v5, /device:TPU:1, one launch (start us, length us, event | category | flops | bytes accessed | tf_op | source)
XLA Modules:
  0.0 139.1 jit_solution(12140201285469155974)
XLA Ops:
  7.2 0.0 all-gather.2.cloned.1.call-start
  7.2 0.7 all-gather.2.cloned.1.call-update
  7.9 3.0 %shard_map.76 = bf16[16,208,128]{2,1,0:T(8,128)(2,1)} custom-call(s32[1,128]{1,0:T(1,128)} %bitcast.15, bf16[128,3072]{1,0:T(8,128)(2,1)} %x_hbm.3, bf16[128,3072]{1,0:T(8,128)(2,1)} %g_hbm.3, f32[8,3072]{1,0:T(8,128)} %bitcast.12), custom_call_target="tpu_custom_call" | custom-call | bytes 1671680 | tf_op jit(solution)/shard_map/pallas_call | solution.py:61
  11.0 0.0 copy-start
  11.0 0.0 copy-start.3
  11.0 19.0 %all_to_all.30.recv_ref = bf16[16,208,128]{2,1,0:T(8,128)(2,1)S(1)} all-to-all(bf16[16,208,128]{2,1,0:T(8,128)(2,1)} %shard_map.76), channel_id=1, replica_groups=mesh['z'=16,'core'=2,'x'=4,'y'=4] {'x','y'}, dimensions={0} | all-to-all | bytes 1703936 | tf_op jit(solution)/shard_map/all_to_all | solution.py:198
  30.0 0.0 copy-done
  30.0 0.0 copy-done.3
  30.0 0.0 copy-start.1
  30.0 0.0 copy-start.4
  30.0 0.6 shard_map.77
  30.7 6.6 %psum.7 = f32[8,192]{1,0:T(8,128)S(1)} all-reduce(f32[8,192]{1,0:T(8,128)S(1)} %shard_map.77), channel_id=1, replica_groups=mesh['z'=16,'core'=2,'x'=4,'y'=4] {'core'}, use_global_device_ids=true, to_apply=%region_0.0 | all-reduce | flops 1536 | bytes 12288 | tf_op jit(solution)/shard_map/psum | solution.py:227
  37.3 26.9 %all_to_all.31 = f32[16,8,192]{2,1,0:T(8,128)S(1)} all-to-all(f32[16,8,192]{2,1,0:T(8,128)S(1)} %broadcast_in_dim.13), channel_id=1, replica_groups=mesh['z'=16,'core'=2,'x'=4,'y'=4] {'z'}, dimensions={0} | all-to-all | bytes 196608 | tf_op jit(solution)/shard_map/all_to_all | solution.py:198
  64.2 10.7 %all_to_all.32.pfull_ref = f32[16,8,192]{2,1,0:T(8,128)S(1)} all-to-all(f32[16,8,192]{2,1,0:T(8,128)S(1)} %broadcast_in_dim.14), channel_id=1, replica_groups=mesh['z'=16,'core'=2,'x'=4,'y'=4] {'x','y'}, dimensions={0} | all-to-all | bytes 196608 | tf_op jit(solution)/shard_map/all_to_all | solution.py:198
  74.8 0.0 copy-done.1
  74.9 0.0 copy-done.4
  74.9 0.0 copy-start.2
  74.9 1.1 copy-done.2
  76.0 2.8 %shard_map.78 = (f32[8,192]{1,0:T(8,128)}, f32[8,192]{1,0:T(8,128)S(1)}, f32[192,128]{1,0:T(8,128)S(1)}) custom-call(f32[16,8,192]{2,1,0:T(8,128)S(1)} %all_to_all.32.pfull_ref, f32[8,192]{1,0:T(8,128)S(1)} %broadcast_multiply_fusion.pown_ref, s32[1,128]{1,0:T(1,128)S(1)} %bitcast.16, bf16[128,3072]{1,0:T(8,128)(2,1)S(1)} %copy-done.2, ...), custom_call_target="tpu_custom_call" | custom-call | bytes 2857472 | tf_op jit(solution)/shard_map/pallas_call | solution.py:61
  78.8 16.9 %all_to_all.33 = f32[32,1,768]{2,1,0:T(1,128)S(1)} all-to-all(f32[32,1,768]{2,1,0:T(1,128)S(1)} %bitcast.14), channel_id=1, replica_groups=mesh['z'=16,'core'=2,'x'=4,'y'=4] {'core','x','y'}, dimensions={0} | all-to-all | bytes 196608 | tf_op jit(solution)/shard_map/all_to_all | solution.py:198
  95.7 0.1 reduce_sum.28
  95.8 15.1 %all_to_all.34 = f32[16,1,768]{2,1,0:T(1,128)S(1)} all-to-all(f32[16,1,768]{2,1,0:T(1,128)S(1)} %broadcast_in_dim.15), channel_id=1, replica_groups=mesh['z'=16,'core'=2,'x'=4,'y'=4] {'z'}, dimensions={0} | all-to-all | bytes 98304 | tf_op jit(solution)/shard_map/all_to_all | solution.py:198
  111.0 0.1 broadcast_in_dim.16
  111.0 13.4 %all_to_all.35 = f32[32,1,768]{2,1,0:T(1,128)S(1)} all-to-all(f32[32,1,768]{2,1,0:T(1,128)S(1)} %broadcast_in_dim.16), channel_id=1, replica_groups=mesh['z'=16,'core'=2,'x'=4,'y'=4] {'core','x','y'}, dimensions={0} | all-to-all | bytes 196608 | tf_op jit(solution)/shard_map/all_to_all | solution.py:198
  124.4 0.7 all-gather.2.cloned.1.call-done.g_hbm
  125.2 7.0 %shard_map.79 = (bf16[192,3072]{1,0:T(8,128)(2,1)}, f32[8,3072]{1,0:T(8,128)}) custom-call(bf16[16,208,128]{2,1,0:T(8,128)(2,1)S(1)} %all_to_all.30.recv_ref, bf16[2048,3072]{1,0:T(8,128)(2,1)} %all-gather.2.cloned.1.call-done.g_hbm, bf16[192,3072]{1,0:T(8,128)(2,1)S(1)} %bitcast.10, f32[8,192]{1,0:T(8,128)S(1)} %get-tuple-element.9.p_ref, ...), custom_call_target="tpu_custom_call" | custom-call | flops 2415919104 | bytes 14942208 | tf_op jit(solution)/shard_map/pallas_call | solution.py:176
  (6 shorter events, 0.1 us)
Async XLA Ops:
  7.2 118.0 %all-gather.2.cloned.1.call-start = ((), (), s32[]{:S(2)}) async-start(), calls=%async_computation.6 | async-start | bytes 13369344 | tf_op jit(solution)/shard_map/all_gather | solution.py:216
  11.0 19.1 %copy-start = (bf16[1,192,3072]{2,1,0:T(8,128)(2,1)S(1)}, bf16[1,192,3072]{2,1,0:T(8,128)(2,1)}, u32[]{:S(2)}) copy-start(bf16[1,192,3072]{2,1,0:T(8,128)(2,1)} %param.8) | copy-start | bytes 3538948
  11.0 19.0 %copy-start.3 = (f32[3072,8]{0,1:T(8,128)S(1)}, f32[3072,8]{0,1:T(8,128)}, u32[]{:S(2)}) copy-start(f32[3072,8]{0,1:T(8,128)} %param.9) | copy-start | bytes 294916
  30.0 44.8 %copy-start.1 = (bf16[128,3072]{1,0:T(8,128)(2,1)S(1)}, bf16[128,3072]{1,0:T(8,128)(2,1)}, u32[]{:S(2)}) copy-start(bf16[128,3072]{1,0:T(8,128)(2,1)} %g_hbm.3) | copy-start | bytes 2359300
  30.0 44.8 %copy-start.4 = (s32[128]{0:T(128)S(1)}, s32[128]{0:T(128)}, u32[]{:S(2)}) copy-start(s32[128]{0:T(128)} %param.5) | copy-start | bytes 1540
  74.9 1.1 copy-start.2
Sparse Core Ops, SparseCore 0:
  11.1 114.0 all-gather.1
